TPU v7x, 32 devices: a whole 2x2x4 slice. The times are simulated.
32 devices in a mesh: dp: 16 (over z, y, x), mp: 2 (over core).
Axes of the slice: x: 2, y: 2, z: 4, core: 2. Of those that a mesh axis runs over, the one named last changes fastest.
Arguments:
- media: bfloat16 [12288, 1024], P('dp'), may hold values from -6 to 6
- latents: bfloat16 [3072, 1024], P('dp'), may hold values from -6 to 6
- patch_rows: int32 [48], P('dp'), may hold values from 128 to 256, as said below
- image_count: int32 [16], P('dp'), may hold values from 1 to 3, as said below
- cotangent: bfloat16 [3072, 1024], P('dp'), may hold values from -6 to 6
- w_query: bfloat16 [2, 1024, 512], P(None, 'dp', 'mp'), may hold values from -0.1875 to 0.1875
- w_key: bfloat16 [2, 1024, 512], P(None, 'dp', 'mp'), may hold values from -0.1875 to 0.1875
- w_value: bfloat16 [2, 1024, 512], P(None, 'dp', 'mp'), may hold values from -0.1875 to 0.1875
- w_out: bfloat16 [2, 512, 1024], P(None, 'mp', 'dp'), may hold values from -1.5 to 1.5
- w_up: bfloat16 [2, 1024, 4096], P(None, 'dp', 'mp'), may hold values from -0.1875 to 0.1875
- w_down: bfloat16 [2, 4096, 1024], P(None, 'mp', 'dp'), may hold values from -0.09375 to 0.09375
- norm_gains: bfloat16 [2, 3, 1024], P(None, None, 'dp'), may hold values from 0.25 to 1.75
- norm_shifts: bfloat16 [2, 3, 1024], P(None, None, 'dp'), may hold values from -3 to 3
Outputs:
- latents_out: bfloat16 [3072, 1024], P('dp')
- media_grad: float32 [12288, 1024], P('dp')
- latents_grad: float32 [3072, 1024], P('dp')
- query_grad: float32 [2, 1024, 512], P(None, 'dp', 'mp')
- key_grad: float32 [2, 1024, 512], P(None, 'dp', 'mp')
- value_grad: float32 [2, 1024, 512], P(None, 'dp', 'mp')
- output_grad: float32 [2, 512, 1024], P(None, 'mp', 'dp')
- up_grad: float32 [2, 1024, 4096], P(None, 'dp', 'mp')
- down_grad: float32 [2, 4096, 1024], P(None, 'mp', 'dp')
- gains_grad: float32 [2, 2, 1024], P(None, None, 'dp')
- shifts_grad: float32 [2, 2, 1024], P(None, None, 'dp')
- feed_norm_grad: float32 [2, 2, 1024], P(None, None, 'dp')
Inputs may be any that keep to these rules, and one draw needn't show every extreme that they name: The first image_count of a device's 3 slots hold images, the others are empty; some device has all 3 in every draw. The first patch_rows of a slot's 256 patch rows are valid; some slot has all 256 in every draw.
All inputs are finite; a program needn't handle non-finite values.
Results may differ from a plain program's by a relative error of at most 0.023.
Values may be sent and summed in bfloat16 or wider, within the bound.
A program may use at most 192 MiB of HBM per device.

v0:
```python
from functools import partial

import jax
import jax.numpy as jnp
from jax import lax
from jax.sharding import PartitionSpec as P

HEAD_DIM = 64
LATENTS = 64
PATCH = 256


NEGATIVE = -1000000000.0


def normalize(values, gain, shift):
    centre = values - jnp.mean(values, -1, keepdims=True)
    spread = jnp.mean(centre * centre, -1, keepdims=True)
    return centre * lax.rsqrt(spread + 1e-05) * gain + shift


def product(left, right):
    return jnp.dot(left, right, preferred_element_type=jnp.float32)


def outer_sum(left, right):
    return lax.dot_general(
        left, right, (((0,), (0,)), ((), ())), preferred_element_type=jnp.float32
    )


def back_product(left, right):
    return lax.dot_general(
        left, right, (((1,), (1,)), ((), ())), preferred_element_type=jnp.float32
    )


def forward_reduce(values):
    return lax.psum(values.astype(jnp.bfloat16), "mp").astype(jnp.float32)


def backward_reduce(values):
    return lax.psum(values.astype(jnp.bfloat16), "mp").astype(jnp.float32)


def key_scores(query_heads, key_heads, key_mask):
    scores = (
        jnp.einsum("iqhd,ikhd->ihqk", query_heads, key_heads, preferred_element_type=jnp.float32)
        * 0.125
    )
    return jnp.where(key_mask[:, None, None, :], scores, NEGATIVE)


def local(
    media,
    latents,
    patch_rows,
    image_count,
    cotangent,
    w_query,
    w_key,
    w_value,
    w_out,
    w_up,
    w_down,
    norm_gains,
    norm_shifts,
):
    images = patch_rows.shape[0]
    width = media.shape[1]
    heads_here = w_query.shape[2] // HEAD_DIM
    layers = w_query.shape[0]
    keys_len = PATCH + LATENTS
    key_mask = jnp.concatenate(
        [
            jnp.arange(PATCH, dtype=jnp.int32)[None, :] < patch_rows[:, None],
            jnp.ones((images, LATENTS), bool),
        ],
        1,
    )
    live = (jnp.arange(images, dtype=jnp.int32) < image_count[0]).astype(jnp.float32)
    live_rows = jnp.repeat(live, LATENTS)[:, None]
    media_full = media.astype(jnp.float32)
    state = latents.astype(jnp.float32)
    saved = []
    for layer in range(layers):
        gathered = (
            lax.all_gather(w_query[layer], "dp", axis=0, tiled=True),
            lax.all_gather(w_key[layer], "dp", axis=0, tiled=True),
            lax.all_gather(w_value[layer], "dp", axis=0, tiled=True),
            lax.all_gather(w_out[layer], "dp", axis=1, tiled=True),
            lax.all_gather(w_up[layer], "dp", axis=0, tiled=True),
            lax.all_gather(w_down[layer], "dp", axis=1, tiled=True),
            lax.all_gather(norm_gains[layer], "dp", axis=1, tiled=True),
            lax.all_gather(norm_shifts[layer], "dp", axis=1, tiled=True),
        )
        full_query, full_key, full_value, full_out, full_up, full_down, gain_rows, shift_rows = (
            gathered
        )
        gains = gain_rows.astype(jnp.float32)
        shifts = shift_rows.astype(jnp.float32)
        media_low = normalize(media_full, gains[0], shifts[0]).astype(jnp.bfloat16)
        latent_low = normalize(state, gains[1], shifts[1]).astype(jnp.bfloat16)
        query = product(latent_low, full_query).astype(jnp.bfloat16)
        joined = jnp.concatenate(
            [media_low.reshape(images, PATCH, width), latent_low.reshape(images, LATENTS, width)], 1
        ).reshape(images * keys_len, width)
        keys = product(joined, full_key).astype(jnp.bfloat16)
        values = product(joined, full_value).astype(jnp.bfloat16)
        scores = key_scores(
            query.reshape(images, LATENTS, heads_here, HEAD_DIM),
            keys.reshape(images, keys_len, heads_here, HEAD_DIM),
            key_mask,
        )
        top = jnp.max(scores, -1, keepdims=True)
        expo = jnp.exp(scores - top)
        total = jnp.sum(expo, -1, keepdims=True)
        probs_low = (expo / total).astype(jnp.bfloat16)
        log_total = top + jnp.log(total)
        mixed = jnp.einsum(
            "ihqk,ikhd->iqhd",
            probs_low,
            values.reshape(images, keys_len, heads_here, HEAD_DIM),
            preferred_element_type=jnp.float32,
        )
        mixed_low = mixed.astype(jnp.bfloat16).reshape(images * LATENTS, heads_here * HEAD_DIM)
        middle = state + forward_reduce(product(mixed_low, full_out))
        hidden_low = normalize(middle, gains[2], shifts[2]).astype(jnp.bfloat16)
        pre_act = product(hidden_low, full_up)
        act_low = jax.nn.gelu(pre_act, approximate=False).astype(jnp.bfloat16)
        kept_weights = None
        saved.append(
            (
                kept_weights,
                state,
                latent_low,
                joined,
                query,
                keys,
                values,
                log_total,
                mixed_low,
                middle,
                hidden_low,
                pre_act,
                act_low,
            )
        )
        state = middle + forward_reduce(product(act_low, full_down))
    result = (state * live_rows).astype(jnp.bfloat16)
    grad_state = cotangent.astype(jnp.float32) * live_rows
    media_part = jnp.zeros_like(media_full)
    grads = [None] * layers
    for layer in reversed(range(layers)):
        (
            kept_weights,
            state_in,
            latent_low,
            joined,
            query,
            keys,
            values,
            log_total,
            mixed_low,
            middle,
            hidden_low,
            pre_act,
            act_low,
        ) = saved[layer]
        weights_now = (
            lax.all_gather(w_query[layer], "dp", axis=0, tiled=True),
            lax.all_gather(w_key[layer], "dp", axis=0, tiled=True),
            lax.all_gather(w_value[layer], "dp", axis=0, tiled=True),
            lax.all_gather(w_out[layer], "dp", axis=1, tiled=True),
            lax.all_gather(w_up[layer], "dp", axis=0, tiled=True),
            lax.all_gather(w_down[layer], "dp", axis=1, tiled=True),
            lax.all_gather(norm_gains[layer], "dp", axis=1, tiled=True),
            lax.all_gather(norm_shifts[layer], "dp", axis=1, tiled=True),
        )
        full_query, full_key, full_value, full_out, full_up, full_down, gain_rows, shift_rows = (
            weights_now
        )
        gains = gain_rows.astype(jnp.float32)
        shifts = shift_rows.astype(jnp.float32)
        down_low = grad_state.astype(jnp.bfloat16)
        grad_down = outer_sum(act_low, down_low)
        grad_act = back_product(down_low, full_down)
        unused, gelu_pull = jax.vjp(partial(jax.nn.gelu, approximate=False), pre_act)
        up_low = gelu_pull(grad_act)[0].astype(jnp.bfloat16)
        grad_up = outer_sum(hidden_low, up_low)
        grad_hidden = backward_reduce(back_product(up_low, full_up))
        unused, norm_pull = jax.vjp(normalize, middle, gains[2], shifts[2])
        grad_middle, gain_feed, shift_feed = norm_pull(grad_hidden)
        grad_middle = grad_middle + grad_state
        out_low = grad_middle.astype(jnp.bfloat16)
        grad_out = outer_sum(mixed_low, out_low)
        grad_mixed = (
            back_product(out_low, full_out)
            .astype(jnp.bfloat16)
            .reshape(images, LATENTS, heads_here, HEAD_DIM)
        )
        query_heads = query.reshape(images, LATENTS, heads_here, HEAD_DIM)
        key_heads = keys.reshape(images, keys_len, heads_here, HEAD_DIM)
        value_heads = values.reshape(images, keys_len, heads_here, HEAD_DIM)
        probs = jnp.exp(key_scores(query_heads, key_heads, key_mask) - log_total)
        probs_low = probs.astype(jnp.bfloat16)
        grad_probs = jnp.einsum(
            "iqhd,ikhd->ihqk", grad_mixed, value_heads, preferred_element_type=jnp.float32
        )
        grad_scores = (
            probs * (grad_probs - jnp.sum(grad_probs * probs, -1, keepdims=True))
        ).astype(jnp.bfloat16)
        grad_values = jnp.einsum(
            "ihqk,iqhd->ikhd", probs_low, grad_mixed, preferred_element_type=jnp.float32
        ).astype(jnp.bfloat16)
        grad_query = (
            jnp.einsum(
                "ihqk,ikhd->iqhd", grad_scores, key_heads, preferred_element_type=jnp.float32
            )
            * 0.125
        ).astype(jnp.bfloat16)
        grad_keys = (
            jnp.einsum(
                "ihqk,iqhd->ikhd", grad_scores, query_heads, preferred_element_type=jnp.float32
            )
            * 0.125
        ).astype(jnp.bfloat16)
        grad_query = grad_query.reshape(images * LATENTS, heads_here * HEAD_DIM)
        grad_keys = grad_keys.reshape(images * keys_len, heads_here * HEAD_DIM)
        grad_values = grad_values.reshape(images * keys_len, heads_here * HEAD_DIM)
        grad_wq = outer_sum(latent_low, grad_query)
        grad_wk = outer_sum(joined, grad_keys)
        grad_wv = outer_sum(joined, grad_values)
        grad_joined = (
            back_product(grad_keys, full_key) + back_product(grad_values, full_value)
        ).reshape(images, keys_len, width)
        grad_latent = backward_reduce(
            back_product(grad_query, full_query)
            + grad_joined[:, PATCH:].reshape(images * LATENTS, width)
        )
        unused, norm_pull = jax.vjp(normalize, state_in, gains[1], shifts[1])
        grad_in, gain_latent, shift_latent = norm_pull(grad_latent)
        grad_state = grad_middle + grad_in
        unused, media_pull = jax.vjp(normalize, media_full, gains[0], shifts[0])
        grad_media_layer, gain_media, shift_media = media_pull(
            grad_joined[:, :PATCH].reshape(images * PATCH, width)
        )
        media_part = media_part + grad_media_layer
        grads[layer] = (
            grad_wq,
            grad_wk,
            grad_wv,
            grad_out,
            grad_up,
            grad_down,
            gain_media,
            shift_media,
            gain_latent,
            shift_latent,
            gain_feed,
            shift_feed,
        )
    media_total, gain_media_all, shift_media_all = (
        lax.psum(media_part.astype(jnp.bfloat16), "mp").astype(jnp.float32),
        lax.psum(jnp.stack([g[6] for g in grads]).astype(jnp.bfloat16), "mp").astype(jnp.float32),
        lax.psum(jnp.stack([g[7] for g in grads]).astype(jnp.bfloat16), "mp").astype(jnp.float32),
    )
    gain_stack = jnp.stack(
        [jnp.stack([gain_media_all[layer], grads[layer][8]]) for layer in range(layers)]
    )
    shift_stack = jnp.stack(
        [jnp.stack([shift_media_all[layer], grads[layer][9]]) for layer in range(layers)]
    )
    feed_stack = jnp.stack(
        [jnp.stack([grads[layer][10], grads[layer][11]]) for layer in range(layers)]
    )
    summed = (
        lax.psum_scatter(jnp.stack([g[0] for g in grads]), "dp", scatter_dimension=1, tiled=True),
        lax.psum_scatter(jnp.stack([g[1] for g in grads]), "dp", scatter_dimension=1, tiled=True),
        lax.psum_scatter(jnp.stack([g[2] for g in grads]), "dp", scatter_dimension=1, tiled=True),
        lax.psum_scatter(jnp.stack([g[3] for g in grads]), "dp", scatter_dimension=2, tiled=True),
        lax.psum_scatter(jnp.stack([g[4] for g in grads]), "dp", scatter_dimension=1, tiled=True),
        lax.psum_scatter(jnp.stack([g[5] for g in grads]), "dp", scatter_dimension=2, tiled=True),
        lax.psum_scatter(gain_stack, "dp", scatter_dimension=2, tiled=True),
        lax.psum_scatter(shift_stack, "dp", scatter_dimension=2, tiled=True),
        lax.psum_scatter(feed_stack, "dp", scatter_dimension=2, tiled=True),
    )
    return (
        result,
        media_total,
        grad_state,
        summed[0],
        summed[1],
        summed[2],
        summed[3],
        summed[4],
        summed[5],
        summed[6],
        summed[7],
        summed[8],
    )


def solution(mesh):
    placed = (
        P("dp", None),
        P("dp", None),
        P("dp"),
        P("dp"),
        P("dp", None),
        P(None, "dp", "mp"),
        P(None, "dp", "mp"),
        P(None, "dp", "mp"),
        P(None, "mp", "dp"),
        P(None, "dp", "mp"),
        P(None, "mp", "dp"),
        P(None, None, "dp"),
        P(None, None, "dp"),
    )
    return jax.shard_map(
        local,
        mesh=mesh,
        in_specs=placed,
        out_specs=(
            P("dp", None),
            P("dp", None),
            P("dp", None),
            P(None, "dp", "mp"),
            P(None, "dp", "mp"),
            P(None, "dp", "mp"),
            P(None, "mp", "dp"),
            P(None, "dp", "mp"),
            P(None, "mp", "dp"),
            P(None, None, "dp"),
            P(None, None, "dp"),
            P(None, None, "dp"),
        ),
        check_vma=False,
    )
```

profile of v0, /device:TPU:0, one launch (start us, length us, event | category | flops | bytes accessed | tf_op | source)
XLA Modules:
  0.0 2373.4 jit_solution(8001984466534271523)
XLA Ops:
  17.0 45.3 %all-gather = bf16[1,3,1024]{1,0,2:T(2,128)(2,1)S(1)} all-gather(bf16[1,3,64]{1,0,2:T(2,128)(2,1)S(1)} %copy.159), channel_id=2, replica_groups=mesh['dp'=16,'mp'=2] {'dp'}, dimensions={2}, use_global_device_ids=true | all-gather | bytes 6528 | tf_op jit(solution)/shard_map/all_gather | solution.py:94
  62.9 10.3 slice_reduce_fusion.7
  73.2 38.8 %all-gather.1 = bf16[1,3,1024]{1,0,2:T(2,128)(2,1)S(1)} all-gather(bf16[1,3,64]{1,0,2:T(2,128)(2,1)S(1)} %copy.160), channel_id=3, replica_groups=mesh['dp'=16,'mp'=2] {'dp'}, dimensions={2}, use_global_device_ids=true | all-gather | bytes 6528 | tf_op jit(solution)/shard_map/all_gather | solution.py:95
  112.5 10.4 slice_reduce_fusion.6
  122.9 40.9 %all-gather.8 = bf16[1,3,1024]{1,0,2:T(2,128)(2,1)S(1)} all-gather(bf16[1,3,64]{1,0,2:T(2,128)(2,1)S(1)} %copy.161), channel_id=10, replica_groups=mesh['dp'=16,'mp'=2] {'dp'}, dimensions={2}, use_global_device_ids=true | all-gather | bytes 6528 | tf_op jit(solution)/shard_map/all_gather | solution.py:94
  164.3 10.3 slice_reduce_fusion.1
  174.6 39.3 %all-gather.9 = bf16[1,3,1024]{1,0,2:T(2,128)(2,1)S(1)} all-gather(bf16[1,3,64]{1,0,2:T(2,128)(2,1)S(1)} %copy.162), channel_id=11, replica_groups=mesh['dp'=16,'mp'=2] {'dp'}, dimensions={2}, use_global_device_ids=true | all-gather | bytes 6528 | tf_op jit(solution)/shard_map/all_gather | solution.py:95
  214.5 10.3 slice_reduce_fusion
  224.7 40.1 %all-gather.5 = bf16[1,256,1024]{1,2,0:T(8,128)(2,1)S(1)} all-gather(bf16[1,256,64]{1,2,0:T(8,128)(2,1)S(1)} %get-tuple-element.122), channel_id=7, replica_groups=mesh['dp'=16,'mp'=2] {'dp'}, dimensions={2}, use_global_device_ids=true | all-gather | bytes 557056 | tf_op jit(solution)/shard_map/all_gather | solution.py:91
  264.8 40.9 %all-gather.2 = bf16[1,1024,256]{2,1,0:T(8,128)(2,1)} all-gather(bf16[1,64,256]{2,1,0:T(8,128)(2,1)S(1)} %get-tuple-element.128), channel_id=4, replica_groups=mesh['dp'=16,'mp'=2] {'dp'}, dimensions={1}, use_global_device_ids=true | all-gather | bytes 557056 | tf_op jit(solution)/shard_map/all_gather | solution.py:90
  305.7 43.0 %all-gather.4 = bf16[1,1024,256]{2,1,0:T(8,128)(2,1)} all-gather(bf16[1,64,256]{2,1,0:T(8,128)(2,1)S(1)} %get-tuple-element.124), channel_id=6, replica_groups=mesh['dp'=16,'mp'=2] {'dp'}, dimensions={1}, use_global_device_ids=true | all-gather | bytes 557056 | tf_op jit(solution)/shard_map/all_gather | solution.py:89
  348.7 38.7 %all-gather.3 = bf16[1,1024,256]{2,1,0:T(8,128)(2,1)S(1)} all-gather(bf16[1,64,256]{2,1,0:T(8,128)(2,1)S(1)} %get-tuple-element.126), channel_id=5, replica_groups=mesh['dp'=16,'mp'=2] {'dp'}, dimensions={1}, use_global_device_ids=true | all-gather | bytes 557056 | tf_op jit(solution)/shard_map/all_gather | solution.py:88
  396.7 3.3 convolution_convert_fusion.5
  412.3 45.0 %all-gather.13 = bf16[1,256,1024]{1,2,0:T(8,128)(2,1)} all-gather(bf16[1,256,64]{1,2,0:T(8,128)(2,1)S(1)} %get-tuple-element.121), channel_id=15, replica_groups=mesh['dp'=16,'mp'=2] {'dp'}, dimensions={2}, use_global_device_ids=true | all-gather | bytes 557056 | tf_op jit(solution)/shard_map/all_gather | solution.py:91
  457.4 42.8 %all-gather.10 = bf16[1,1024,256]{2,1,0:T(8,128)(2,1)} all-gather(bf16[1,64,256]{2,1,0:T(8,128)(2,1)S(1)} %get-tuple-element.127), channel_id=12, replica_groups=mesh['dp'=16,'mp'=2] {'dp'}, dimensions={1}, use_global_device_ids=true | all-gather | bytes 557056 | tf_op jit(solution)/shard_map/all_gather | solution.py:90
  502.7 8.4 multiply_convert_fusion.1
  511.1 60.4 %all-gather.23.cloned.1.call-done = bf16[1,2048,1024]{1,2,0:T(8,128)(2,1)} async-done(((bf16[1,2048,64]{1,2,0:T(8,128)(2,1)}), bf16[1,2048,1024]{1,2,0:T(8,128)(2,1)}) %all-gather.23.cloned.1.call-update) | async-done | bytes 4194320 | tf_op jit(solution)/shard_map/all_gather | solution.py:93
  571.5 4.5 fusion.64
  576.1 43.8 %all-gather.12 = bf16[1,1024,256]{2,1,0:T(8,128)(2,1)} all-gather(bf16[1,64,256]{2,1,0:T(8,128)(2,1)S(1)} %copy-done.82), channel_id=14, replica_groups=mesh['dp'=16,'mp'=2] {'dp'}, dimensions={1}, use_global_device_ids=true | all-gather | bytes 557056 | tf_op jit(solution)/shard_map/all_gather | solution.py:89
  619.9 41.4 %all-gather.11 = bf16[1,1024,256]{2,1,0:T(8,128)(2,1)} all-gather(bf16[1,64,256]{2,1,0:T(8,128)(2,1)S(1)} %copy-done.81), channel_id=13, replica_groups=mesh['dp'=16,'mp'=2] {'dp'}, dimensions={1}, use_global_device_ids=true | all-gather | bytes 557056 | tf_op jit(solution)/shard_map/all_gather | solution.py:88
  671.4 3.3 convolution_convert_fusion.3
  677.4 3.1 copy.123
  689.1 14.0 all-reduce.19.cloned.1.call-done
  706.1 57.6 %all-gather.25.cloned.1.call-done = bf16[1,1024,2048]{2,1,0:T(8,128)(2,1)} async-done(((bf16[1,64,2048]{2,1,0:T(8,128)(2,1)}), bf16[1,1024,2048]{2,1,0:T(8,128)(2,1)}) %all-gather.25.cloned.1.call-update) | async-done | bytes 4194320 | tf_op jit(solution)/shard_map/all_gather | solution.py:92
  763.8 8.2 multiply_convert_fusion
  772.0 69.3 %all-gather.27.cloned.1.call-done = bf16[1,2048,1024]{1,2,0:T(8,128)(2,1)} async-done(((bf16[1,2048,64]{1,2,0:T(8,128)(2,1)}), bf16[1,2048,1024]{1,2,0:T(8,128)(2,1)}) %all-gather.27.cloned.1.call-update) | async-done | bytes 4194320 | tf_op jit(solution)/shard_map/all_gather | solution.py:93
  841.3 4.9 add_convert_fusion.2
  850.9 15.7 all-reduce.21.cloned.1.call-done
  900.5 19.8 all-reduce.23.cloned.1.call-done
  927.3 3.9 add_convert_fusion.1
  935.1 4.8 fusion.70
  939.8 14.4 all-reduce.25.cloned.1.call-done
  977.7 4.1 slice_reduce_fusion.12
  982.2 4.0 fusion.33
  999.9 6.6 pad_maximum_fusion.1
  1006.5 25.6 %copy.142 = f32[2,2048,1024]{1,0,2:T(2,128)} copy(f32[2,2048,1024]{2,1,0:T(8,128)} %pad_maximum_fusion.1) | data formatting | bytes 33554432 | tf_op jit(solution)/shard_map/stack | solution.py:283
  1051.6 3.1 pad_maximum_fusion.5
  1054.7 4.1 copy.141
  1077.7 6.1 pad_maximum_fusion
  1085.7 32.8 %reduce-scatter.26.cloned.1.call-done = f32[64,4]{1,0:T(8,128)} async-done(((f32[1024,4]{1,0:T(8,128)}), f32[64,4]{1,0:T(8,128)}) %reduce-scatter.26.cloned.1.call-update) | async-done | bytes 1040
  1119.9 3.5 convert_element_type.289
  1125.6 68.1 %reduce-scatter.24.cloned.1.call-done = f32[64,4]{1,0:T(8,128)} async-done(((f32[1024,4]{1,0:T(8,128)}), f32[64,4]{1,0:T(8,128)}) %reduce-scatter.24.cloned.1.call-update) | async-done | bytes 1040
  1195.2 73.6 %reduce-scatter.22.cloned.1.call-done = f32[64,4]{1,0:T(8,128)} async-done(((f32[1024,4]{1,0:T(8,128)}), f32[64,4]{1,0:T(8,128)}) %reduce-scatter.22.cloned.1.call-update) | async-done | bytes 1040
  1270.4 505.1 %all-reduce.27.cloned.1.call-done = (f32[2,256,1024]{1,0,2:T(2,128)}, f32[2,2048,1024]{1,0,2:T(2,128)}) async-done(((f32[2,256,1024]{1,0,2:T(2,128)}, f32[2,2048,1024]{1,0,2:T(2,128)}), (f32[2,256,1024]{1,0,2:T(2,128)}, f32[2,2048,1024]{1,0,2:T(2,128)})) %all-reduce.27.cloned.1.call-update) | async-done | bytes 18874384
  1779.9 78.1 %reduce-scatter.14.cloned.1.call-done = f32[2,64,256]{2,1,0:T(8,128)} async-done(((f32[2,1024,256]{2,1,0:T(8,128)}), f32[2,64,256]{2,1,0:T(8,128)}) %reduce-scatter.14.cloned.1.call-update) | async-done | bytes 131088 | tf_op jit(solution)/shard_map/reduce_scatter | solution.py:278
  1858.0 80.7 %reduce-scatter.16.cloned.1.call-done = f32[2,64,256]{2,1,0:T(8,128)} async-done(((f32[2,1024,256]{2,1,0:T(8,128)}), f32[2,64,256]{2,1,0:T(8,128)}) %reduce-scatter.16.cloned.1.call-update) | async-done | bytes 131088 | tf_op jit(solution)/shard_map/reduce_scatter | solution.py:279
  1938.8 80.5 %reduce-scatter.18.cloned.1.call-done = f32[2,64,256]{2,1,0:T(8,128)} async-done(((f32[2,1024,256]{2,1,0:T(8,128)}), f32[2,64,256]{2,1,0:T(8,128)}) %reduce-scatter.18.cloned.1.call-update) | async-done | bytes 131088 | tf_op jit(solution)/shard_map/reduce_scatter | solution.py:280
  2019.2 346.6 %reduce-scatter.20.cloned.1.call-done = f32[2,64,2048]{2,1,0:T(8,128)} async-done(((f32[2,1024,2048]{2,1,0:T(8,128)}), f32[2,64,2048]{2,1,0:T(8,128)}) %reduce-scatter.20.cloned.1.call-update) | async-done | bytes 1048592 | tf_op jit(solution)/shard_map/reduce_scatter | solution.py:282
  (532 shorter events, 195.2 us)
Async XLA Ops:
  8.0 492.1 %all-reduce.15.cloned.1.call-start = ((), (), s32[]{:S(2)}) async-start(), calls=%async_computation.7 | async-start | bytes 786432 | tf_op jit(solution)/shard_map/psum | solution.py:39
  10.0 377.4 %copy-start.106 = (f32[192]{0:T(256)}, f32[192]{0:T(256)S(1)}, u32[]{:S(2)}) copy-start(f32[192]{0:T(256)S(1)} %broadcast_multiply_fusion.4) | copy-start | bytes 2308
  11.3 376.1 %copy-start.125 = (f32[192]{0:T(256)}, f32[192]{0:T(256)S(1)}, u32[]{:S(2)}) copy-start(f32[192]{0:T(256)S(1)} %fusion.140) | copy-start | bytes 2308
  15.2 373.6 %copy-start.94 = (f32[768]{0:T(1024)}, f32[768]{0:T(1024)S(1)}, u32[]{:S(2)}) copy-start(f32[768]{0:T(1024)S(1)} %fusion.139) | copy-start | bytes 9220
  73.2 314.3 %copy-start.85 = (f32[1024]{0:T(1024)}, f32[1024]{0:T(1024)S(1)}, u32[]{:S(2)}) copy-start(f32[1024]{0:T(1024)S(1)} %get-tuple-element.83) | copy-start | bytes 12292
  174.6 214.3 %copy-start.83 = (f32[1024]{0:T(1024)}, f32[1024]{0:T(1024)S(1)}, u32[]{:S(2)}) copy-start(f32[1024]{0:T(1024)S(1)} %get-tuple-element.78) | copy-start | bytes 12292
  214.5 173.0 %copy-start = (bf16[192,1024]{1,0:T(8,128)(2,1)S(1)}, bf16[192,1024]{1,0:T(8,128)(2,1)}, u32[]{:S(2)}) copy-start(bf16[192,1024]{1,0:T(8,128)(2,1)} %param.14) | copy-start | bytes 1179652
  264.8 143.4 %copy-start.33 = (bf16[1,256,1024]{1,2,0:T(8,128)(2,1)}, bf16[1,256,1024]{1,2,0:T(8,128)(2,1)S(1)}, u32[]{:S(2)}) copy-start(bf16[1,256,1024]{1,2,0:T(8,128)(2,1)S(1)} %all-gather.5) | copy-start | bytes 1572868
  388.8 17.0 copy-start.63
  396.7 9.1 copy-start.23
  409.4 93.3 %all-gather.21.cloned.1.call-start = ((), (), s32[]{:S(2)}) async-start(), calls=%async_computation.17 | async-start | bytes 4456448 | tf_op jit(solution)/shard_map/all_gather | solution.py:92
  411.4 160.2 %all-gather.23.cloned.1.call-start = ((), (), s32[]{:S(2)}) async-start(), calls=%async_computation.18 | async-start | bytes 4456448 | tf_op jit(solution)/shard_map/all_gather | solution.py:93
  412.3 90.5 %copy-start.87 = (f32[1024]{0:T(1024)S(1)}, f32[1024]{0:T(1024)}, u32[]{:S(2)}) copy-start(f32[1024]{0:T(1024)} %get-tuple-element.85) | copy-start | bytes 12292
  412.3 249.0 %all-reduce.17.cloned.1.call-start = ((), (), s32[]{:S(2)}) async-start(), calls=%async_computation.8 | async-start | bytes 786432 | tf_op jit(solution)/shard_map/psum | solution.py:39
  501.4 9.7 copy-start.103
  502.7 8.4 copy-start.140
  502.7 8.4 copy-start.114
  511.1 64.9 %copy-start.67 = (bf16[192,2048]{1,0:T(8,128)(2,1)}, bf16[192,2048]{1,0:T(8,128)(2,1)S(1)}, u32[]{:S(2)}) copy-start(bf16[192,2048]{1,0:T(8,128)(2,1)S(1)} %get-tuple-element.109) | copy-start | bytes 2359300
  571.5 48.4 %copy-start.81 = (bf16[1,64,256]{2,1,0:T(8,128)(2,1)S(1)}, bf16[1,64,256]{2,1,0:T(8,128)(2,1)}, u32[]{:S(2)}) copy-start(bf16[1,64,256]{2,1,0:T(8,128)(2,1)} %get-tuple-element.125) | copy-start | bytes 98308
  576.0 127.0 %all-reduce.19.cloned.1.call-start = ((), (), s32[]{:S(2)}) async-start(), calls=%async_computation.9 | async-start | bytes 786432 | tf_op jit(solution)/shard_map/psum | solution.py:39
  619.9 43.0 %copy-start.90 = (f32[1024]{0:T(1024)S(1)}, f32[1024]{0:T(1024)}, u32[]{:S(2)}) copy-start(f32[1024]{0:T(1024)} %get-tuple-element.77) | copy-start | bytes 12292
  619.9 43.0 %copy-start.124 = (f32[1024]{0:T(1024)S(1)}, f32[1024]{0:T(1024)}, u32[]{:S(2)}) copy-start(f32[1024]{0:T(1024)} %get-tuple-element.80) | copy-start | bytes 12292
  664.0 16.4 copy-start.65
  671.4 9.1 copy-start.25
  686.3 77.4 %all-gather.25.cloned.1.call-start = ((), (), s32[]{:S(2)}) async-start(), calls=%async_computation.19 | async-start | bytes 4456448 | tf_op jit(solution)/shard_map/all_gather | solution.py:92
  686.9 154.4 %all-gather.27.cloned.1.call-start = ((), (), s32[]{:S(2)}) async-start(), calls=%async_computation.20 | async-start | bytes 4456448 | tf_op jit(solution)/shard_map/all_gather | solution.py:93
  687.7 179.0 %all-reduce.21.cloned.1.call-start = ((), (), s32[]{:S(2)}) async-start(), calls=%async_computation.10 | async-start | bytes 786432 | tf_op jit(solution)/shard_map/psum | solution.py:43
  849.4 70.9 %all-reduce.23.cloned.1.call-start = ((), (), s32[]{:S(2)}) async-start(), calls=%async_computation.11 | async-start | bytes 786432 | tf_op jit(solution)/shard_map/psum | solution.py:43
  900.5 53.7 %all-reduce.25.cloned.1.call-start = ((), (), s32[]{:S(2)}) async-start(), calls=%async_computation.12 | async-start | bytes 786432 | tf_op jit(solution)/shard_map/psum | solution.py:43
  934.4 106.3 %all-reduce.29.cloned.1.call-start = ((), (), s32[]{:S(2)}) async-start(), calls=%async_computation.25 | async-start | bytes 4718592 | tf_op jit(solution)/shard_map/psum | solution.py:39
  935.1 19.2 copy-start.9
  935.1 19.2 copy-start.104
  935.1 20.6 copy-start.141
  935.1 20.6 copy-start.115
  993.8 124.6 %reduce-scatter.26.cloned.1.call-start = ((), (), s32[]{:S(2)}) async-start(), calls=%async_computation.23 | async-start | bytes 557056
  1006.5 25.7 %copy-start.131 = (f32[1024]{0:T(1024)S(1)}, f32[1024]{0:T(1024)}, u32[]{:S(2)}) copy-start(f32[1024]{0:T(1024)} %get-tuple-element.72) | copy-start | bytes 12292
  1006.5 25.7 %copy-start.132 = (f32[1024]{0:T(1024)S(1)}, f32[1024]{0:T(1024)}, u32[]{:S(2)}) copy-start(f32[1024]{0:T(1024)} %get-tuple-element.89) | copy-start | bytes 12292
  1006.5 25.7 %copy-start.133 = (f32[1024]{0:T(1024)S(1)}, f32[1024]{0:T(1024)}, u32[]{:S(2)}) copy-start(f32[1024]{0:T(1024)} %get-tuple-element.68) | copy-start | bytes 12292
  1006.5 25.7 %copy-start.134 = (f32[1024]{0:T(1024)S(1)}, f32[1024]{0:T(1024)}, u32[]{:S(2)}) copy-start(f32[1024]{0:T(1024)} %get-tuple-element.88) | copy-start | bytes 12292
  1032.1 7.0 copy-start.13
  1032.1 7.1 copy-start.74
  1040.5 153.2 %reduce-scatter.24.cloned.1.call-start = ((), (), s32[]{:S(2)}) async-start(), calls=%async_computation.22 | async-start | bytes 557056
  1047.5 221.3 %reduce-scatter.22.cloned.1.call-start = ((), (), s32[]{:S(2)}) async-start(), calls=%async_computation.21 | async-start | bytes 557056
  1051.5 724.0 %all-reduce.27.cloned.1.call-start = ((), (), s32[]{:S(2)}) async-start(), calls=%async_computation.24 | async-start | bytes 37748736
  1058.8 799.2 %reduce-scatter.14.cloned.1.call-start = ((), (), s32[]{:S(2)}) async-start(), calls=%async_computation.13 | async-start | bytes 2228224 | tf_op jit(solution)/shard_map/reduce_scatter | solution.py:278
  1062.0 876.7 %reduce-scatter.16.cloned.1.call-start = ((), (), s32[]{:S(2)}) async-start(), calls=%async_computation.14 | async-start | bytes 2228224 | tf_op jit(solution)/shard_map/reduce_scatter | solution.py:279
  1067.9 951.4 %reduce-scatter.18.cloned.1.call-start = ((), (), s32[]{:S(2)}) async-start(), calls=%async_computation.15 | async-start | bytes 2228224 | tf_op jit(solution)/shard_map/reduce_scatter | solution.py:280
  1073.7 1292.0 %reduce-scatter.20.cloned.1.call-start = ((), (), s32[]{:S(2)}) async-start(), calls=%async_computation.16 | async-start | bytes 17825792 | tf_op jit(solution)/shard_map/reduce_scatter | solution.py:282
  (122 other events, 300.4 us)
Sparse Core Ops, SparseCore 0:
  409.5 16.8 all-reduce.14
  576.2 17.0 all-reduce.16
  686.5 16.5 all-reduce.18
  849.5 17.0 all-reduce.20
  900.6 19.6 all-reduce.22
  934.5 19.6 all-reduce.24
  993.9 22.9 all-reduce.28
Sparse Core Ops, SparseCore 1:
  413.6 79.5 all-gather.20
  496.8 74.7 all-gather.22
  690.0 73.7 all-gather.24
  766.9 74.3 all-gather.26
  1040.6 77.7 reduce-scatter.25
  1120.7 73.0 reduce-scatter.23
  1195.9 72.9 reduce-scatter.21
  1275.1 500.3 all-reduce.26
  1778.3 79.6 reduce-scatter.13
  1861.0 77.7 reduce-scatter.15
  1941.6 77.6 reduce-scatter.17
  2022.2 343.5 reduce-scatter.19
where the time goes:
time: 2390 us; the launch traced here: 2370 us
  waiting for transfers between devices  1520 us (64%)
  blocking collectives  503 us (21%)
  local copies, waits for them, and re-layouts  169 us (7%)
  matrix products  86 us (4%)
  other arithmetic  77.2 us (3%)
    unnamed x23, waiting for transfers between devices  681 us
    reduce_scatter x1, waiting for transfers between devices, local(): lax.psum_scatter(jnp.stack([g[4] for g in grads]), 'dp', scatter_dimensio...  347 us
    all_gather x2, waiting for transfers between devices, local(): lax.all_gather(w_down[layer], 'dp', axis=1, tiled=True)  130 us
    all_gather x2, blocking collectives, local(): lax.all_gather(w_key[layer], 'dp', axis=0, tiled=True)  86.8 us
    all_gather x2, blocking collectives, local(): lax.all_gather(norm_gains[layer], 'dp', axis=1, tiled=True)  86.2 us
    all_gather x2, blocking collectives, local(): lax.all_gather(w_out[layer], 'dp', axis=1, tiled=True)  85.1 us
    all_gather x2, blocking collectives, local(): lax.all_gather(w_value[layer], 'dp', axis=0, tiled=True)  83.7 us
    reduce_scatter x1, waiting for transfers between devices, local(): lax.psum_scatter(jnp.stack([g[1] for g in grads]), 'dp', scatter_dimensio...  80.7 us
  transfers between devices with their start and end apart: 19, of which 15 were waited for; matrix products, arithmetic and copies ran while one was open for 5% of the time, Pallas kernels for 0%

commit v1 on v0

--- a/solution.py
+++ b/solution.py
@@ -3,6 +3,8 @@
 import jax
 import jax.numpy as jnp
 from jax import lax
+from jax.experimental import pallas as pl
+from jax.experimental.pallas import tpu as pltpu
 from jax.sharding import PartitionSpec as P
 
 HEAD_DIM = 64
@@ -301,7 +303,825 @@
     )
 
 
+MESH = pl.DeviceIdType.MESH
+F32 = jnp.float32
+BF16 = jnp.bfloat16
+SLOTS = 3
+HEADS_HERE = 4
+PLANE = 4
+ROWS = SLOTS * LATENTS
+HALF = ROWS // 2
+WIDTH = 1024
+KEYS = PATCH + LATENTS
+HEAD_COLS = HEADS_HERE * HEAD_DIM
+UNITS = 512
+COPIES = 200
+
+
+class Copies:
+    def __init__(self, send_sems, recv_sems):
+        self.send_sems, self.recv_sems = send_sems, recv_sems
+        self.used = 0
+        self.sending = []
+
+    def start(self, source, target, device):
+        copy = pltpu.make_async_remote_copy(
+            src_ref=source,
+            dst_ref=target,
+            send_sem=self.send_sems.at[self.used],
+            recv_sem=self.recv_sems.at[self.used],
+            device_id=device,
+            device_id_type=MESH,
+        )
+        self.used += 1
+        copy.start()
+        self.sending.append(copy)
+        return copy
+
+    def sent(self, copies):
+        for copy in copies:
+            copy.wait_send()
+            self.sending = [kept for kept in self.sending if kept is not copy]
+
+
+def matmul(left, right):
+    return jnp.dot(left, right, preferred_element_type=F32)
+
+
+def matmul_nt(left, right):
+    return lax.dot_general(left, right, (((1,), (1,)), ((), ())), preferred_element_type=F32)
+
+
+def matmul_tn(left, right):
+    return lax.dot_general(left, right, (((0,), (0,)), ((), ())), preferred_element_type=F32)
+
+
+def loop(count, body):
+    def step(index, carry):
+        body(index)
+        return carry
+
+    lax.fori_loop(0, count, step, 0)
+
+
+def centred(values):
+    centre = values - jnp.mean(values, -1, keepdims=True)
+    scale = lax.rsqrt(jnp.mean(centre * centre, -1, keepdims=True) + 1e-05)
+    return centre * scale, scale
+
+
+def norm_back(grad, gain, unit, scale):
+    inner = grad * gain
+    return scale * (
+        inner
+        - jnp.mean(inner, -1, keepdims=True)
+        - unit * jnp.mean(inner * unit, -1, keepdims=True)
+    )
+
+
+def column_sums(values):
+    return jnp.sum(values, 0, keepdims=True)
+
+
+def fused_kernel(
+    patch_rows,
+    image_count,
+    media,
+    latents,
+    cotangent,
+    vectors,
+    w_attn,
+    w_up,
+    w_down_t,
+    out_latents,
+    out_media,
+    out_state,
+    out_attn,
+    out_up,
+    out_down_t,
+    out_vectors,
+    AW,
+    FW,
+    VG,
+    GS,
+    J,
+    X,
+    Y,
+    Q,
+    KV,
+    O,
+    PR,
+    H,
+    GP,
+    G,
+    DY,
+    DU,
+    ZP,
+    PS,
+    PRECV,
+    TS,
+    TR,
+    AS,
+    AR,
+    DX,
+    DH,
+    DV,
+    DAB,
+    DQ,
+    DKV,
+    RF1,
+    RF2,
+    RF3,
+    RA1A,
+    RA1B,
+    RA2A,
+    RA2B,
+    RA3,
+    RA4,
+    VS,
+    VR,
+    MASK,
+    send_sems,
+    recv_sems,
+    local_sems,
+):
+    me = lax.axis_index("dp")
+    half = lax.axis_index("mp")
+    z, c = me // 4, me % 4
+    zh, zl = z // 2, z % 2
+    y, x = c // 2, c % 2
+    columns = (c, y * 2 + 1 - x, (1 - y) * 2 + x, 3 - c)
+    plane = tuple((z * 4 + column, half) for column in columns)
+    near = ((zh * 2 + 1 - zl) * 4 + c, half)
+    far = (((1 - zh) * 2 + zl) * 4 + c, half)
+    sibling = (me, 1 - half)
+    copies = Copies(send_sems, recv_sems)
+    mine = pl.ds(pl.multiple_of(half * HALF, 32), HALF)
+    other = pl.ds(pl.multiple_of((1 - half) * HALF, 32), HALF)
+    first = jnp.where(half == 0, 1.0, 0.0).astype(F32)
+
+    barrier = pltpu.get_barrier_semaphore()
+    for step in range(1, 16):
+        pl.semaphore_signal(barrier, inc=1, device_id=((me + step) % 16, half), device_id_type=MESH)
+    pl.semaphore_signal(barrier, inc=1, device_id=sibling, device_id_type=MESH)
+    pl.semaphore_wait(barrier, 16)
+
+
+    def unit_columns(index):
+        return pl.ds(pl.multiple_of(columns[index] * UNITS, UNITS), UNITS)
+
+    vector_copies = [
+        copies.start(vectors, VG.at[me], ((me + step) % 16, half)) for step in range(1, 16)
+    ]
+    local_copies = []
+    for layer in range(2):
+        for index, (source, target) in enumerate(
+            (
+                (w_attn.at[layer], AW.at[layer, zh, zl, y, x]),
+                (w_up.at[layer, :, unit_columns(0)], FW.at[layer, zh, zl, c, :, 0:UNITS]),
+                (w_down_t.at[layer, :, unit_columns(0)], FW.at[layer, zh, zl, c, :, UNITS:]),
+            )
+        ):
+            copy = pltpu.make_async_copy(source, target, local_sems.at[layer * 3 + index])
+            copy.start()
+            local_copies.append(copy)
+
+    def feed_scatter(layer):
+        started = []
+        for source, part in ((w_up, pl.ds(0, UNITS)), (w_down_t, pl.ds(UNITS, UNITS))):
+            for index in (1, 2, 3):
+                started.append(
+                    copies.start(
+                        source.at[layer, :, unit_columns(index)],
+                        FW.at[layer, zh, zl, c, :, part],
+                        plane[index],
+                    )
+                )
+        return started
+
+    def feed_far(layer, part):
+        block = FW.at[layer, zh, zl, :, :, part]
+        return copies.start(block, block, far)
+
+    def feed_near(layer, part):
+        block = FW.at[layer, :, zl, :, :, part]
+        return copies.start(block, block, near)
+
+    def attn_far(layer):
+        return copies.start(w_attn.at[layer], AW.at[layer, zh, zl, y, x], far)
+
+    def attn_near(layer):
+        block = AW.at[layer, :, zl, y, x]
+        return copies.start(block, block, near)
+
+    def attn_plane_first(layer):
+        block_a = AW.at[layer, :, :, y, x, :, 0:512]
+        block_b = AW.at[layer, :, :, y, x, :, 512:]
+        return [copies.start(block_a, block_a, plane[1]), copies.start(block_b, block_b, plane[2])]
+
+    def attn_plane_second(layer):
+        block_a = AW.at[layer, :, :, y, :, :, 0:512]
+        block_b = AW.at[layer, :, :, :, x, :, 512:]
+        return [copies.start(block_a, block_a, plane[2]), copies.start(block_b, block_b, plane[1])]
+
+    def arrived(started):
+        for copy in started if isinstance(started, list) else [started]:
+            copy.wait_recv()
+
+    up_part, down_part = pl.ds(0, UNITS), pl.ds(UNITS, UNITS)
+    attn0 = attn_far(0)
+    scatter0 = feed_scatter(0)
+
+    head_row = lax.broadcasted_iota(jnp.int32, (HEAD_COLS, HEAD_COLS), 0) // HEAD_DIM
+    head_column = lax.broadcasted_iota(jnp.int32, (HEAD_COLS, HEAD_COLS), 1) // HEAD_DIM
+    MASK[...] = jnp.where(head_row == head_column, 1.0, 0.0).astype(F32)
+    VG[me] = vectors[...]
+    VS[...] = jnp.zeros_like(VS)
+
+    def load_state(slot):
+        rows = pl.ds(pl.multiple_of(slot * LATENTS, LATENTS), LATENTS)
+        X[0, rows, :] = latents[rows, :].astype(F32)
+        live = jnp.where(slot < image_count[0], 1.0, 0.0).astype(F32)
+        grad = cotangent[rows, :].astype(F32) * live
+        DX[rows, :] = grad
+        DY[1, 0, rows, :] = grad.astype(BF16)
+
+    loop(SLOTS, load_state)
+    arrived(vector_copies)
+    for tile in range(8):
+        GS[:, tile * 128 : tile * 128 + 128] = VG[2 * tile].astype(F32) + VG[2 * tile + 1].astype(F32)
+
+    def gain(layer, which):
+        return GS[layer * 3 + which : layer * 3 + which + 1, :]
+
+    def shift(layer, which):
+        return GS[6 + layer * 3 + which : 7 + layer * 3 + which, :]
+
+    def media_norm(index):
+        rows = pl.ds(pl.multiple_of(index * 64, 64), 64)
+        unit, _ = centred(media[rows, :].astype(F32))
+        slot, part = index // 4, index % 4
+        keys = pl.ds(pl.multiple_of(part * 64, 64), 64)
+        for layer in range(2):
+            J[layer, slot, keys, :] = (unit * gain(layer, 0) + shift(layer, 0)).astype(BF16)
+
+    def latent_norm(layer):
+        def body(slot):
+            rows = pl.ds(pl.multiple_of(slot * LATENTS, LATENTS), LATENTS)
+            unit, _ = centred(X[layer, rows, :])
+            J[layer, slot, PATCH:, :] = (unit * gain(layer, 1) + shift(layer, 1)).astype(BF16)
+
+        loop(SLOTS, body)
+
+    loop(4, media_norm)
+    for copy in local_copies:
+        copy.wait()
+    arrived(attn0)
+    attn0 = attn_near(0)
+    loop(4, lambda index: media_norm(index + 4))
+    arrived(scatter0)
+    feed0_up = feed_far(0, up_part)
+    arrived(attn0)
+    attn0 = attn_plane_first(0)
+    loop(4, lambda index: media_norm(index + 8))
+    latent_norm(0)
+    arrived(attn0)
+    attn0 = attn_plane_second(0)
+    arrived(feed0_up)
+    feed0_up = feed_near(0, up_part)
+    feed0_down = feed_far(0, down_part)
+    scatter1 = feed_scatter(1)
+    arrived(attn0)
+
+    def attn_weight(layer, low, high):
+        return AW[layer, :, :, :, :, :, low:high].reshape(WIDTH, high - low)
+
+    def feed_weight(layer, low, high):
+        return FW[layer, :, :, :, :, low:high].reshape(WIDTH, high - low)
+
+    def stacked(value):
+        return (jnp.concatenate([value.astype(F32)] * HEADS_HERE, 0) * MASK[...]).astype(BF16)
+
+    def unstacked(value):
+        return jnp.sum((value * MASK[...]).reshape(HEADS_HERE, LATENTS, HEAD_COLS), 0)
+
+    def attention(layer):
+        def body(slot):
+            KV[layer, slot] = matmul(J[layer, slot], attn_weight(layer, 256, 768)).astype(BF16)
+            query = matmul(J[layer, slot, PATCH:, :], attn_weight(layer, 0, 256)).astype(BF16)
+            Q[layer, slot] = query
+            scores = matmul_nt(stacked(query), KV[layer, slot, :, 0:256]) * 0.125
+            key = lax.broadcasted_iota(jnp.int32, (HEAD_COLS, KEYS), 1)
+            scores = jnp.where((key >= PATCH) | (key < patch_rows[slot]), scores, NEGATIVE)
+            expo = jnp.exp(scores - jnp.max(scores, -1, keepdims=True))
+            probs = expo / jnp.sum(expo, -1, keepdims=True)
+            PR[layer, slot] = probs
+            mixed = unstacked(matmul(probs.astype(BF16), KV[layer, slot, :, 256:512]))
+            O[layer, slot] = mixed.astype(BF16)
+
+        loop(SLOTS, body)
+        AS[...] = matmul_nt(
+            O[layer].reshape(ROWS, HEAD_COLS), attn_weight(layer, 768, 1024)
+        ).astype(BF16)
+        return copies.start(AS, AR, sibling)
+
+    def after_attention(layer, exchange):
+        arrived(exchange)
+
+        def body(slot):
+            rows = pl.ds(pl.multiple_of(slot * LATENTS, LATENTS), LATENTS)
+            middle = X[layer, rows, :] + (AS[rows, :].astype(F32) + AR[rows, :].astype(F32))
+            Y[layer, rows, :] = middle
+            unit, _ = centred(middle)
+            H[layer, 0, rows, :] = (unit * gain(layer, 2) + shift(layer, 2)).astype(BF16)
+
+        loop(SLOTS, body)
+        copies.sent([exchange])
+
+    def spread(buffer, layer):
+        block = buffer.at[layer, 0, mine]
+        return [
+            copies.start(block, buffer.at[layer, index, mine], plane[index]) for index in (1, 2, 3)
+        ]
+
+    def hand_over(buffer, layer, index, started):
+        arrived(started[index - 1])
+        block = buffer.at[layer, index, mine]
+        return copies.start(block, block, sibling)
+
+    def feed_forward(layer, compute, buffer, started, way):
+        pair = [None] * 4
+        away = []
+
+        def send_away(index):
+            arrived(pair[index])
+            TS[index - 1] = (ZP[index, mine, :] + PRECV[way, index].astype(F32)).astype(BF16)
+            away.append(copies.start(TS.at[index - 1], TR.at[way, index - 1], plane[index]))
+
+        handed = [None] * 4
+        for index in range(4):
+            if index > 0:
+                if index == 1:
+                    handed[1] = hand_over(buffer, layer, 1, started)
+                    handed[2] = hand_over(buffer, layer, 2, started)
+                if index == 3:
+                    handed[3] = hand_over(buffer, layer, 3, started)
+                arrived(handed[index])
+            compute(layer, index)
+            PS[index] = ZP[index, other, :].astype(BF16)
+            pair[index] = copies.start(PS.at[index], PRECV.at[way, index], sibling)
+            if index >= 2:
+                send_away(index - 1)
+        send_away(3)
+        arrived(pair[0])
+        return pair, away + handed[1:]
+
+    def feed_sum(way, pair, away):
+        arrived(away[:3])
+        total = ZP[0, mine, :] + PRECV[way, 0].astype(F32)
+        for index in range(3):
+            total = total + TR[way, index].astype(F32)
+        copies.sent(pair + away)
+        return total
+
+    def forward_block(layer, index):
+        pre_act = matmul(H[layer, index], feed_weight(layer, 0, UNITS))
+        bell = 0.5 * (1.0 + lax.erf(pre_act * 0.7071067811865476))
+        GP[layer, index] = bell + pre_act * jnp.exp(-0.5 * pre_act * pre_act) * 0.3989422804014327
+        act = (pre_act * bell).astype(BF16)
+        G[layer, index] = act
+        ZP[index] = matmul_nt(act, feed_weight(layer, UNITS, 2 * UNITS))
+
+    def backward_block(layer, index):
+        grad_act = matmul(DY[layer, index], feed_weight(layer, UNITS, 2 * UNITS))
+        up_low = (grad_act * GP[layer, index]).astype(BF16)
+        DU[index] = up_low
+        ZP[index] = matmul_nt(up_low, feed_weight(layer, 0, UNITS))
+
+    exchange = attention(0)
+    arrived(feed0_up)
+    arrived(feed0_down)
+    feed0_down = feed_near(0, down_part)
+    attn1 = attn_far(1)
+    after_attention(0, exchange)
+    started = spread(H, 0)
+    arrived(attn1)
+    attn1 = attn_near(1)
+    arrived(scatter1)
+    feed1_up = feed_far(1, up_part)
+    arrived(feed0_down)
+    pair, away = feed_forward(0, forward_block, H, started, 0)
+    arrived(attn1)
+    attn1 = attn_plane_first(1)
+    arrived(feed1_up)
+    feed1_up = feed_near(1, up_part)
+    feed1_down = feed_far(1, down_part)
+    X[1, mine, :] = Y[0, mine, :] + feed_sum(0, pair, away)
+    swap = copies.start(X.at[1, mine], X.at[1, mine], sibling)
+    arrived(attn1)
+    attn1 = attn_plane_second(1)
+    arrived(swap)
+    latent_norm(1)
+    arrived(attn1)
+
+    exchange = attention(1)
+    arrived(feed1_up)
+    arrived(feed1_down)
+    feed1_down = feed_near(1, down_part)
+    after_attention(1, exchange)
+    started = spread(H, 1)
+    grad_started = spread(DY, 1)
+    arrived(feed1_down)
+    pair, away = feed_forward(1, forward_block, H, started, 0)
+    X[2, mine, :] = Y[1, mine, :] + feed_sum(0, pair, away)
+    swap = copies.start(X.at[2, mine], X.at[2, mine], sibling)
+    arrived(swap)
+
+    def store_result(slot):
+        rows = pl.ds(pl.multiple_of(slot * LATENTS, LATENTS), LATENTS)
+        live = jnp.where(slot < image_count[0], 1.0, 0.0).astype(F32)
+        out_latents[rows, :] = (X[2, rows, :] * live).astype(BF16)
+
+    loop(SLOTS, store_result)
+
+    def add_into(target, received):
+        target[...] = (target[...].astype(F32) + received[...].astype(F32)).astype(BF16)
+
+    def feed_grads(layer):
+        def body(index):
+            cols = pl.ds(pl.multiple_of(index * 256, 256), 256)
+            for low, left, right in ((UNITS, DY, G.at[layer]), (0, H, DU)):
+                product_ = matmul_tn(
+                    left[layer, :, :, cols].reshape(4 * ROWS, 256),
+                    right[...].reshape(4 * ROWS, UNITS),
+                )
+                FW[layer, index // 2, index % 2, :, :, low : low + UNITS] = product_.astype(
+                    BF16
+                ).reshape(4, 64, UNITS)
+
+        loop(4, body)
+
+    def feed_sum_near(layer, part):
+        return copies.start(
+            FW.at[layer, :, 1 - zl, :, :, part], RF1.at[layer, :, :, :, part], near
+        )
+
+    def feed_sum_far(layer, part, started):
+        arrived(started)
+
+        def body(index):
+            add_into(FW.at[layer, index // 4, zl, index % 4, :, part], RF1.at[layer, index // 4, index % 4, :, part])
+
+        loop(8, body)
+        return copies.start(FW.at[layer, 1 - zh, zl, :, :, part], RF2.at[layer, :, :, part], far)
+
+    def feed_sum_plane(layer, part, started):
+        arrived(started)
+
+        def body(index):
+            add_into(FW.at[layer, zh, zl, index, :, part], RF2.at[layer, index, :, part])
+
+        loop(4, body)
+        return [
+            copies.start(
+                FW.at[layer, zh, zl, columns[index], :, part],
+                RF3.at[layer, index - 1, :, part],
+                plane[index],
+            )
+            for index in (1, 2, 3)
+        ]
+
+    def feed_sum_end(layer, part, target, started):
+        target[layer, :, unit_columns(0)] = FW[layer, zh, zl, c, :, part].astype(F32)
+        for index in (1, 2, 3):
+            arrived(started[index - 1])
+            target[layer, :, unit_columns(index)] = RF3[layer, index - 1, :, part].astype(F32)
+
+    def attn_sum_first(layer):
+        return [
+            copies.start(AW.at[layer, :, :, 1 - y, :, :, 0:512], RA1A.at[layer], plane[2]),
+            copies.start(AW.at[layer, :, :, :, 1 - x, :, 512:], RA1B.at[layer], plane[1]),
+        ]
+
+    def attn_sum_second(layer, started):
+        arrived(started)
+
+        def body(index):
+            high, low = index // 2, index % 2
+            for side in range(2):
+                add_into(AW.at[layer, high, low, y, side, :, 0:512], RA1A.at[layer, high, low, side])
+                add_into(AW.at[layer, high, low, side, x, :, 512:], RA1B.at[layer, high, low, side])
+
+        loop(4, body)
+        return [
+            copies.start(AW.at[layer, :, :, y, 1 - x, :, 0:512], RA2A.at[layer], plane[1]),
+            copies.start(AW.at[layer, :, :, 1 - y, x, :, 512:], RA2B.at[layer], plane[2]),
+        ]
+
+    def attn_sum_near(layer, started):
+        arrived(started)
+
+        def body(index):
+            high, low = index // 2, index % 2
+            add_into(AW.at[layer, high, low, y, x, :, 0:512], RA2A.at[layer, high, low])
+            add_into(AW.at[layer, high, low, y, x, :, 512:], RA2B.at[layer, high, low])
+
+        loop(4, body)
+        return copies.start(AW.at[layer, :, 1 - zl, y, x], RA3.at[layer], near)
+
+    def attn_sum_far(layer, started):
+        arrived(started)
+        for high in range(2):
+            add_into(AW.at[layer, high, zl, y, x], RA3.at[layer, high])
+        return copies.start(AW.at[layer, 1 - zh, zl, y, x], RA4.at[layer], far)
+
+    def attn_sum_end(layer, started):
+        arrived(started)
+        out_attn[layer] = AW[layer, zh, zl, y, x].astype(F32) + RA4[layer].astype(F32)
+
+    def swap_feed(layer, pair, away):
+        DH[mine, :] = feed_sum(1, pair, away)
+        swap = copies.start(DH.at[mine], DH.at[mine], sibling)
+        arrived(swap)
+        copies.sent([swap])
+
+    def middle_back(layer):
+        def body(slot, sums):
+            rows = pl.ds(pl.multiple_of(slot * LATENTS, LATENTS), LATENTS)
+            unit, scale = centred(Y[layer, rows, :])
+            grad = DH[rows, :]
+            grad_middle = DX[rows, :] + norm_back(grad, gain(layer, 2), unit, scale)
+            DV[rows, :] = grad_middle
+            DAB[rows, :] = grad_middle.astype(BF16)
+            return sums[0] + column_sums(grad * unit), sums[1] + column_sums(grad)
+
+        zero = jnp.zeros((1, WIDTH), F32)
+        gain_sum, shift_sum = lax.fori_loop(0, SLOTS, body, (zero, zero))
+        VS[8 + layer * 2 : 9 + layer * 2, :] = gain_sum * first
+        VS[9 + layer * 2 : 10 + layer * 2, :] = shift_sum * first
+
+    def attention_back(layer):
+        def body(slot):
+            rows = pl.ds(pl.multiple_of(slot * LATENTS, LATENTS), LATENTS)
+            grad_mixed = matmul(DAB[rows, :], attn_weight(layer, 768, 1024)).astype(BF16)
+            grads = stacked(grad_mixed)
+            probs = PR[layer, slot]
+            grad_probs = matmul_nt(grads, KV[layer, slot, :, 256:512])
+            grad_scores = (
+                probs * (grad_probs - jnp.sum(grad_probs * probs, -1, keepdims=True))
+            ).astype(BF16)
+            DKV[slot, :, 256:512] = matmul_tn(probs.astype(BF16), grads).astype(BF16)
+            queries = stacked(Q[layer, slot])
+            DKV[slot, :, 0:256] = (matmul_tn(grad_scores, queries) * 0.125).astype(BF16)
+            DQ[slot] = (
+                unstacked(matmul(grad_scores, KV[layer, slot, :, 0:256])) * 0.125
+            ).astype(BF16)
+            AS[rows, :] = (
+                matmul_nt(DQ[slot], attn_weight(layer, 0, 256))
+                + matmul_nt(DKV[slot, PATCH:, :], attn_weight(layer, 256, 768))
+            ).astype(BF16)
+
+        loop(SLOTS, body)
+        return copies.start(AS, AR, sibling)
+
+    def state_back(layer, exchange):
+        arrived(exchange)
+
+        def body(slot, sums):
+            rows = pl.ds(pl.multiple_of(slot * LATENTS, LATENTS), LATENTS)
+            unit, scale = centred(X[layer, rows, :])
+            grad = AS[rows, :].astype(F32) + AR[rows, :].astype(F32)
+            grad_in = DV[rows, :] + norm_back(grad, gain(layer, 1), unit, scale)
+            if layer > 0:
+                DX[rows, :] = grad_in
+                DY[layer - 1, 0, rows, :] = grad_in.astype(BF16)
+            else:
+                out_state[rows, :] = grad_in
+            return sums[0] + column_sums(grad * unit), sums[1] + column_sums(grad)
+
+        zero = jnp.zeros((1, WIDTH), F32)
+        gain_sum, shift_sum = lax.fori_loop(0, SLOTS, body, (zero, zero))
+        VS[layer * 2 + 1 : layer * 2 + 2, :] = gain_sum * first
+        VS[layer * 2 + 5 : layer * 2 + 6, :] = shift_sum * first
+        copies.sent([exchange])
+
+    def media_back(layer):
+        def body(index, sums):
+            slot, part = index // 2, index % 2
+            keys = pl.ds(pl.multiple_of(part * 128, 128), 128)
+            rows = pl.ds(pl.multiple_of(index * 128, 128), 128)
+            grad = matmul_nt(DKV[slot, keys, :], attn_weight(layer, 256, 768))
+            unit, scale = centred(media[rows, :].astype(F32))
+            piece = norm_back(grad, gain(layer, 0), unit, scale)
+            if layer == 1:
+                out_media[rows, :] = piece
+            else:
+                out_media[rows, :] = out_media[rows, :] + piece
+            return sums[0] + column_sums(grad * unit), sums[1] + column_sums(grad)
+
+        zero = jnp.zeros((1, WIDTH), F32)
+        gain_sum, shift_sum = lax.fori_loop(0, 6, body, (zero, zero))
+        VS[layer * 2 : layer * 2 + 1, :] = gain_sum
+        VS[layer * 2 + 4 : layer * 2 + 5, :] = shift_sum
+
+    def attn_grads(layer):
+        def body(index):
+            cols = pl.ds(pl.multiple_of(index * 256, 256), 256)
+            high, low = index // 2, index % 2
+            query_part = matmul_tn(
+                J[layer, :, PATCH:, cols].reshape(ROWS, 256), DQ[...].reshape(ROWS, HEAD_COLS)
+            )
+            AW[layer, high, low, :, :, :, 0:256] = query_part.astype(BF16).reshape(2, 2, 64, 256)
+            key_part = matmul_tn(
+                J[layer, :, :, cols].reshape(SLOTS * KEYS, 256), DKV[...].reshape(SLOTS * KEYS, 512)
+            )
+            AW[layer, high, low, :, :, :, 256:768] = key_part.astype(BF16).reshape(2, 2, 64, 512)
+            out_part = matmul_tn(DAB[:, cols], O[layer].reshape(ROWS, HEAD_COLS))
+            AW[layer, high, low, :, :, :, 768:1024] = out_part.astype(BF16).reshape(2, 2, 64, 256)
+
+        loop(4, body)
+
+    copies.sent(list(copies.sending))
+    pair, away = feed_forward(1, backward_block, DY, grad_started, 1)
+    feed_grads(1)
+    down1 = feed_sum_near(1, down_part)
+    up1 = feed_sum_near(1, up_part)
+    swap_feed(1, pair, away)
+    middle_back(1)
+    exchange = attention_back(1)
+    down1 = feed_sum_far(1, down_part, down1)
+    state_back(1, exchange)
+    started = spread(DY, 0)
+    media_back(1)
+    attn_grads(1)
+    attn1 = attn_sum_first(1)
+    up1 = feed_sum_far(1, up_part, up1)
+
+    pair, away = feed_forward(0, backward_block, DY, started, 1)
+    down1 = feed_sum_plane(1, down_part, down1)
+    attn1 = attn_sum_second(1, attn1)
+    feed_grads(0)
+    down0 = feed_sum_near(0, down_part)
+    up0 = feed_sum_near(0, up_part)
+    swap_feed(0, pair, away)
+    middle_back(0)
+    exchange = attention_back(0)
+    up1 = feed_sum_plane(1, up_part, up1)
+    attn1 = attn_sum_near(1, attn1)
+    down0 = feed_sum_far(0, down_part, down0)
+    state_back(0, exchange)
+    media_back(0)
+    attn_grads(0)
+    attn0 = attn_sum_first(0)
+
+    vector_sums = [
+        copies.start(
+            VS.at[:, pl.ds(pl.multiple_of((((me + step) % 16) // 2) * 128, 128), 128)],
+            VR.at[step],
+            ((me + step) % 16, half),
+        )
+        for step in range(1, 16)
+    ]
+
+    def media_low(index):
+        rows = pl.ds(pl.multiple_of(index * 192, 192), 192)
+        DY[1, index] = out_media[rows, :].astype(BF16)
+
+    loop(4, media_low)
+    media_swap = copies.start(DY.at[1], H.at[1], sibling)
+    attn1 = attn_sum_far(1, attn1)
+    up0 = feed_sum_far(0, up_part, up0)
+    feed_sum_end(1, down_part, out_down_t, down1)
+    feed_sum_end(1, up_part, out_up, up1)
+    attn0 = attn_sum_second(0, attn0)
+    attn_sum_end(1, attn1)
+    down0 = feed_sum_plane(0, down_part, down0)
+    arrived(media_swap)
+
+    def media_sum(index):
+        rows = pl.ds(pl.multiple_of(index * 192, 192), 192)
+        out_media[rows, :] = DY[1, index].astype(F32) + H[1, index].astype(F32)
+
+    loop(4, media_sum)
+    attn0 = attn_sum_near(0, attn0)
+    up0 = feed_sum_plane(0, up_part, up0)
+    arrived(vector_sums)
+    total = VS[:, pl.ds(pl.multiple_of((me // 2) * 128, 128), 128)]
+    for step in range(1, 16):
+        total = total + VR[step]
+    VR[0] = total
+    vector_swap = copies.start(VR.at[0], VR.at[16], sibling)
+    attn0 = attn_sum_far(0, attn0)
+    feed_sum_end(0, down_part, out_down_t, down0)
+    feed_sum_end(0, up_part, out_up, up0)
+    arrived(vector_swap)
+    out_vectors[...] = VR[0] + VR[16]
+    attn_sum_end(0, attn0)
+    copies.sent(list(copies.sending))
+
+
+def fused(media, latents, patch_rows, image_count, cotangent, w_query, w_key, w_value, w_out, w_up, w_down, norm_gains, norm_shifts):
+    w_attn = jnp.concatenate([w_query, w_key, w_value, jnp.swapaxes(w_out, 1, 2)], 2)
+    w_down_t = jnp.swapaxes(w_down, 1, 2)
+    piece = norm_gains.shape[2]
+    vectors = jnp.concatenate([norm_gains.reshape(6, piece), norm_shifts.reshape(6, piece)], 0)
+    vectors = jnp.pad(vectors, ((0, 4), (0, 0)))
+    odd = lax.axis_index("dp") % 2 == 1
+    blank = jnp.zeros_like(vectors)
+    vectors = jnp.concatenate([jnp.where(odd, blank, vectors), jnp.where(odd, vectors, blank)], 1)
+
+    vmem = pl.BlockSpec(memory_space=pltpu.VMEM)
+    smem = pl.BlockSpec(memory_space=pltpu.SMEM)
+    anywhere = pl.BlockSpec(memory_space=pl.ANY)
+
+    def shape(dims, kind):
+        return jax.ShapeDtypeStruct(dims, kind)
+
+    results = pl.pallas_call(
+        fused_kernel,
+        name="resampler",
+        out_shape=[
+            shape((ROWS, WIDTH), BF16),
+            shape((SLOTS * PATCH, WIDTH), F32),
+            shape((ROWS, WIDTH), F32),
+            shape((2, 64, WIDTH), F32),
+            shape((2, 64, 4 * UNITS), F32),
+            shape((2, 64, 4 * UNITS), F32),
+            shape((16, 128), F32),
+        ],
+        in_specs=[smem, smem, vmem, vmem, vmem, vmem, anywhere, anywhere, anywhere],
+        out_specs=[vmem] * 7,
+        scratch_shapes=[
+            pltpu.VMEM((2, 2, 2, 2, 2, 64, 1024), BF16),
+            pltpu.VMEM((2, 2, 2, 4, 64, 1024), BF16),
+            pltpu.VMEM((16, 16, 128), BF16),
+            pltpu.VMEM((16, WIDTH), F32),
+            pltpu.VMEM((2, SLOTS, KEYS, WIDTH), BF16),
+            pltpu.VMEM((3, ROWS, WIDTH), F32),
+            pltpu.VMEM((2, ROWS, WIDTH), F32),
+            pltpu.VMEM((2, SLOTS, LATENTS, HEAD_COLS), BF16),
+            pltpu.VMEM((2, SLOTS, KEYS, 2 * HEAD_COLS), BF16),
+            pltpu.VMEM((2, SLOTS, LATENTS, HEAD_COLS), BF16),
+            pltpu.VMEM((2, SLOTS, HEAD_COLS, KEYS), F32),
+            pltpu.VMEM((2, PLANE, ROWS, WIDTH), BF16),
+            pltpu.VMEM((2, PLANE, ROWS, UNITS), F32),
+            pltpu.VMEM((2, PLANE, ROWS, UNITS), BF16),
+            pltpu.VMEM((2, PLANE, ROWS, WIDTH), BF16),
+            pltpu.VMEM((PLANE, ROWS, UNITS), BF16),
+            pltpu.VMEM((PLANE, ROWS, WIDTH), F32),
+            pltpu.VMEM((PLANE, HALF, WIDTH), BF16),
+            pltpu.VMEM((2, PLANE, HALF, WIDTH), BF16),
+            pltpu.VMEM((3, HALF, WIDTH), BF16),
+            pltpu.VMEM((2, 3, HALF, WIDTH), BF16),
+            pltpu.VMEM((ROWS, WIDTH), BF16),
+            pltpu.VMEM((ROWS, WIDTH), BF16),
+            pltpu.VMEM((ROWS, WIDTH), F32),
+            pltpu.VMEM((ROWS, WIDTH), F32),
+            pltpu.VMEM((ROWS, WIDTH), F32),
+            pltpu.VMEM((ROWS, WIDTH), BF16),
+            pltpu.VMEM((SLOTS, LATENTS, HEAD_COLS), BF16),
+            pltpu.VMEM((SLOTS, KEYS, 2 * HEAD_COLS), BF16),
+            pltpu.VMEM((2, 2, 4, 64, 1024), BF16),
+            pltpu.VMEM((2, 4, 64, 1024), BF16),
+            pltpu.VMEM((2, 3, 64, 1024), BF16),
+            pltpu.VMEM((2, 2, 2, 2, 64, 512), BF16),
+            pltpu.VMEM((2, 2, 2, 2, 64, 512), BF16),
+            pltpu.VMEM((2, 2, 2, 64, 512), BF16),
+            pltpu.VMEM((2, 2, 2, 64, 512), BF16),
+            pltpu.VMEM((2, 2, 64, 1024), BF16),
+            pltpu.VMEM((2, 64, 1024), BF16),
+            pltpu.VMEM((16, WIDTH), F32),
+            pltpu.VMEM((17, 16, 128), F32),
+            pltpu.VMEM((HEAD_COLS, HEAD_COLS), F32),
+            pltpu.SemaphoreType.DMA((COPIES,)),
+            pltpu.SemaphoreType.DMA((COPIES,)),
+            pltpu.SemaphoreType.DMA((6,)),
+        ],
+        compiler_params=pltpu.CompilerParams(
+            collective_id=0, has_side_effects=True, vmem_limit_bytes=66 * 2**20 - 2**21
+        ),
+        cost_estimate=pl.CostEstimate(flops=18 * 10**9, bytes_accessed=20 * 10**6, transcendentals=10**6),
+    )(patch_rows, image_count, media, latents, cotangent, vectors, w_attn, w_up, w_down_t)
+    out_latents, out_media, out_state, attn, up, down_t, sums = results
+    sums = jnp.where(odd, sums[:, piece:], sums[:, :piece])
+    return (
+        out_latents,
+        out_media,
+        out_state,
+        attn[:, :, 0:256],
+        attn[:, :, 256:512],
+        attn[:, :, 512:768],
+        jnp.swapaxes(attn[:, :, 768:], 1, 2),
+        up,
+        jnp.swapaxes(down_t, 1, 2),
+        sums[0:4].reshape(2, 2, piece),
+        sums[4:8].reshape(2, 2, piece),
+        sums[8:12].reshape(2, 2, piece),
+    )
+
+
 def solution(mesh):
+    body = fused if (mesh.shape["dp"], mesh.shape["mp"]) == (16, 2) else local
     placed = (
         P("dp", None),
         P("dp", None),
@@ -318,7 +1138,7 @@
         P(None, None, "dp"),
     )
     return jax.shard_map(
-        local,
+        body,
         mesh=mesh,
         in_specs=placed,
         out_specs=(

time: 2390 us -> 287 us (0.12)
  waiting for transfers between devices: 1520 us -> 0 us
  blocking collectives: 503 us -> 0 us
  Pallas kernels: 0 us -> 269 us
  local copies, waits for them, and re-layouts: 169 us -> 12.6 us
  matrix products: 86 us -> 0 us
  other arithmetic: 77.2 us -> 3.2 us
    unnamed x23 -> x0, waiting for transfers between devices: 681 us -> none
    reduce_scatter x4 -> x0, waiting for transfers between devices: 586 us -> none  [the longest x1 347 us: local(): lax.psum_scatter(jnp.stack([g[4] for g in grads]), 'dp', scatter_dimensio...]
    all_gather x12 -> x0, blocking collectives: 500 us -> none  [the longest x2 86.8 us: local(): lax.all_gather(w_key[layer], 'dp', axis=0, tiled=True)]
    pallas_call x0 -> x1, Pallas kernels: none -> 269 us  [fused(): pl.pallas_call(fused_kernel, name='resampler', out_shape=[shape((ROWS, WI...]
    all_gather x4 -> x0, waiting for transfers between devices: 187 us -> none  [the longest x2 130 us: local(): lax.all_gather(w_down[layer], 'dp', axis=1, tiled=True)]
    dot_general x48 -> x0, matrix products: 86 us -> none  [the longest x12 36.4 us: product(): return jnp.dot(left, right, preferred_element_type=jnp.float32)]
    psum x7 -> x0, waiting for transfers between devices: 63.9 us -> none  [the longest x3 49.9 us: backward_reduce(): return lax.psum(values.astype(jnp.bfloat16), 'mp').astype(jnp.float32)]
    slice x16 -> x1, local copies, waits for them, and re-layouts: 47.7 us -> 0.59 us  [fused(): sums[8:12].reshape(2, 2, piece)]
  transfers between devices with their start and end apart: 19 -> 0, of which waited for: 15 -> 0; matrix products, arithmetic and copies ran while one was open for 5% -> 0% of each run, Pallas kernels for 0% -> 0%
where the time goes in v1:
time: 287 us; the launch traced here: 286 us
  Pallas kernels  269 us (94%)
  local copies, waits for them, and re-layouts  12.6 us (4%)
  other arithmetic  3.2 us (1%)
    pallas_call x1, Pallas kernels, fused(): pl.pallas_call(fused_kernel, name='resampler', out_shape=[shape((ROWS, WI...  269 us
    unnamed x13, local copies, waits for them, and re-layouts  10.1 us

profile of v1, /device:TPU:0, one launch (start us, length us, event | category | flops | bytes accessed | tf_op | source)
XLA Modules:
  0.0 286.4 jit_solution(15566156718635525433)
XLA Ops:
  1.3 0.7 copy.27
  2.0 0.7 copy.28
  2.7 0.7 pad_maximum_fusion.1.vectors
  3.4 1.7 pad_maximum_fusion.w_attn
  5.1 269.3 %resampler.1 = (bf16[192,1024]{1,0:T(8,128)(2,1)}, f32[768,1024]{1,0:T(8,128)}, f32[192,1024]{1,0:T(8,128)}, f32[2,64,1024]{2,1,0:T(8,128)}, f32[2,64,2048]{2,1,...) custom-call(s32[3]{0:T(128)} %patch_rows.1, s32[1]{0:T(128)S(6)} %copy.34.image_count, bf16[768,1024]{1,0:T(8,128)(2,1)} %media.1, ...), custom_call_target="tpu_custom_call" | custom-call | flops 17999998976 | bytes 20000000 | tf_op jit(solution)/shard_map/resampler/pallas_call | solution.py:1040
  274.3 0.8 slice_select_fusion
  275.2 0.6 fusion.3
  275.8 1.9 slice_bitcast_fusion
  277.7 1.8 copy.35
  279.4 0.0 copy-start.2
  279.4 0.0 copy-start.1
  279.5 4.1 %copy.36 = f32[768,1024]{1,0:T(8,128)} copy(f32[768,1024]{1,0:T(8,128)} %get-tuple-element.48) | data formatting | bytes 6291456
  283.6 0.0 copy-done.2
  283.6 0.0 copy-start
  283.6 0.9 copy.37
  284.4 0.0 copy-done.1
  284.4 1.0 copy.38
  285.4 0.0 copy-done
  285.4 1.0 copy.39
  (3 shorter events, 0.1 us)
Async XLA Ops:
  279.4 4.1 %copy-start.2 = (f32[192,1024]{1,0:T(8,128)S(1)}, f32[192,1024]{1,0:T(8,128)}, u32[]{:S(2)}) copy-start(f32[192,1024]{1,0:T(8,128)} %get-tuple-element.49) | copy-start | bytes 2359300
  279.4 5.0 %copy-start.1 = (f32[2,64,2048]{2,1,0:T(8,128)S(1)}, f32[2,64,2048]{2,1,0:T(8,128)}, u32[]{:S(2)}) copy-start(f32[2,64,2048]{2,1,0:T(8,128)} %get-tuple-element.54) | copy-start | bytes 3145732
  283.6 1.9 copy-start
